TPU v7x, 512 devices: a whole 4x8x8 slice. The times are simulated.
512 devices in a mesh: section: 32 (over z_lo, y, core), tp: 16 (over x, z_hi).
Axes of the slice: x: 4, y: 8, z: 8 (z_hi: 4, z_lo: 2; z = z_hi * 2 + z_lo), core: 2. Of those that a mesh axis runs over, the one named last changes fastest.
Arguments:
- block_weights: bfloat16 [32, 3072, 4, 2048], P(None, 'section', None, 'tp'), may hold values from -0.109375 to 0.109375
- modulation: float32 [32, 3, 3072], P('section'), may hold values from -4 to 4
- inflow: bfloat16 [32, 512, 3072], P('section', None, 'tp'), may hold values from -6 to 6
- stale_cache: bfloat16 [32, 2, 2048, 2048], P('section', None, None, 'tp'), may hold values from -120 to 120
- patch_index: int32 [32], P('section'), may hold values from 0 to 3
- assignment: int32 [32], replicated, may hold values from 0 to 31, each once
Outputs:
- outflow: bfloat16 [32, 512, 3072], P('section', None, 'tp')
All inputs are finite; a program needn't handle non-finite values.
Results may differ from a plain program's by a relative error of at most 0.022.
Values may be sent and summed in bfloat16 or wider, within the bound.
A program may use at most 64 MiB of HBM per device.

v0:
```python
import jax
import jax.numpy as jnp
from jax import lax
from jax.sharding import PartitionSpec as P

HD = 128


def passed_along(block, axis, distance):
    devices = range(lax.axis_size(axis))
    route = [((i - distance) % len(devices), i) for i in devices]
    return lax.ppermute(block, axis, route)


def local(block_weights, modulation, inflow, stale_cache, patch_index, assignment):
    blocks = assignment.shape[0]
    section_ids = jnp.arange(blocks, dtype=jnp.int32)
    owner_table = (assignment[None, :] == section_ids[:, None]).astype(jnp.int32)
    inverse = jnp.sum(owner_table * section_ids[None, :], axis=1)
    ordered = jnp.take(block_weights, inverse, axis=0)
    resident = lax.all_to_all(ordered, "section", split_axis=0, concat_axis=1, tiled=True)[0]
    width = resident.shape[0]
    inner_dev = resident.shape[2]
    heads_dev = inner_dev // HD
    patch = inflow.shape[1]
    seq_len = stale_cache.shape[2]
    tokens = lax.all_gather(inflow, "tp", axis=2, tiled=True)[0].astype(jnp.float32)
    center = jnp.mean(tokens, axis=1, keepdims=True)
    spread = jnp.mean((tokens - center) ** 2, axis=1, keepdims=True)
    normed = (tokens - center) * lax.rsqrt(spread + 1e-06)
    normed = (normed * (1.0 + modulation[0, 0]) + modulation[0, 1]).astype(jnp.bfloat16)
    projected = jnp.dot(
        normed, resident[:, :3, :].reshape(width, 3 * inner_dev), preferred_element_type=jnp.float32
    )
    projected = projected.astype(jnp.bfloat16).reshape(patch, 3, inner_dev)
    start = patch_index[0] * patch
    zero_index = jnp.zeros((), jnp.int32)
    keys_all = lax.dynamic_update_slice(stale_cache[0, 0], projected[:, 1], (start, zero_index))
    values_all = lax.dynamic_update_slice(stale_cache[0, 1], projected[:, 2], (start, zero_index))
    query = projected[:, 0].reshape(patch, heads_dev, HD)
    scores = jnp.einsum(
        "phd,shd->hps",
        query,
        keys_all.reshape(seq_len, heads_dev, HD),
        preferred_element_type=jnp.float32,
    )
    scores = scores / jnp.sqrt(jnp.float32(HD))
    highest = jnp.max(scores, axis=2, keepdims=True)
    expo = jnp.exp(scores - highest)
    probabilities = (expo / jnp.sum(expo, axis=2, keepdims=True)).astype(jnp.bfloat16)
    attended = jnp.einsum(
        "hps,shd->phd",
        probabilities,
        values_all.reshape(seq_len, heads_dev, HD),
        preferred_element_type=jnp.float32,
    )
    attended = attended.astype(jnp.bfloat16).reshape(patch, inner_dev)
    partial_value = jnp.dot(attended, resident[:, 3, :].T, preferred_element_type=jnp.float32)
    share = width // lax.axis_size("tp")
    offset = lax.axis_index("tp") * share
    summed = lax.psum(partial_value.astype(jnp.bfloat16), "tp").astype(jnp.float32)
    mixed = lax.dynamic_slice_in_dim(summed, offset, share, 1)
    gate_part = lax.dynamic_slice_in_dim(modulation[0, 2], offset, share, 0)
    result = (inflow[0].astype(jnp.float32) + gate_part * mixed).astype(jnp.bfloat16)
    return passed_along(result[None], "section", 1)


def solution(mesh):
    placed = (
        P(None, "section", None, "tp"),
        P("section", None, None),
        P("section", None, "tp"),
        P("section", None, None, "tp"),
        P("section"),
        P(),
    )
    return jax.shard_map(
        local, mesh=mesh, in_specs=placed, out_specs=P("section", None, "tp"), check_vma=False
    )
```

profile of v0, /device:TPU:1, one launch (start us, length us, event | category | flops | bytes accessed | tf_op | source)
XLA Modules:
  0.0 360.7 jit_solution(14583519188262189904)
XLA Ops:
  6.5 0.7 all-gather.2.cloned.1.call-update
  7.3 1.0 select_reduce_fusion
  8.4 4.7 %gather_fusion = bf16[32,96,4,128]{3,2,1,0:T(4,128)(2,1)} fusion(bf16[32,96,4,128]{3,2,1,0:T(4,128)(2,1)S(1)} %copy-done, s32[1024]{0:T(1024)S(1)} %pad_clamp_fusion), kind=kCustom, calls=%fused_computation | custom fusion | bytes 6291584 | tf_op jit(solution)/shard_map/jit(_take)/gather | solution.py:20
  13.1 5.0 %broadcast_select_fusion = bf16[32,96,4,128]{3,2,1,0:T(4,128)(2,1)} fusion(bf16[32,96,4,128]{3,2,1,0:T(4,128)(2,1)} %gather_fusion, pred[32]{0:T(512)(128)(4,1)S(1)} %compare_and_fusion), kind=kLoop, calls=%fused_computation.22 | loop fusion | flops 1572864 | bytes 6291488 | tf_op jit(solution)/shard_map/jit(_take)/select_n | solution.py:20
  18.1 11.4 %all-to-all-start = ((bf16[32,96,4,128]{3,2,1,0:T(4,128)(2,1)}), bf16[32,96,4,128]{3,2,1,0:T(4,128)(2,1)}, u32[]{:S(2)}, u32[]{:S(2)}) async-start(bf16[32,96,4,128]{3,2,1,0:T(4,128)(2,1)} %broadcast_select_fusion), calls=%async_computation | async-start | bytes 6291456 | tf_op jit(solution)/shard_map/all_to_all | solution.py:21
  30.4 2.3 slice_bitcast_fusion.2
  32.7 81.5 %all-gather.2.cloned.1.call-done = bf16[1,512,3072]{1,2,0:T(8,128)(2,1)} async-done(((bf16[1,512,192]{1,2,0:T(8,128)(2,1)}), bf16[1,512,3072]{1,2,0:T(8,128)(2,1)}) %all-gather.2.cloned.1.call-update) | async-done | bytes 3145744 | tf_op jit(solution)/shard_map/all_gather | solution.py:27
  114.2 2.5 convert_reduce_fusion
  117.0 0.9 fusion.6
  117.9 2.3 copy.20
  120.3 1.6 copy-done.3
  121.9 1.5 slice.43
  123.5 4.3 %copy.21 = bf16[3072,3,128]{0,2,1:T(8,128)(2,1)} copy(bf16[3072,3,128]{2,0,1:T(8,128)(2,1)} %slice.43) | data formatting | bytes 4718592 | tf_op jit(solution)/shard_map/slice | solution.py:33
  127.8 4.1 %fusion.16 = bf16[512,384]{0,1:T(8,128)(2,1)S(1)} fusion(bf16[3072,384]{0,1:T(8,128)(2,1)} %bitcast.58, bf16[1,512,3072]{1,2,0:T(8,128)(2,1)} %all-gather.2.cloned.1.call-done, f32[3072]{0:T(1024)S(1)} %bitcast.61, f32[3072]{0:T(1024)S(1)} %bitcast.62, f32[512]{0:T(512)S(1)} %add_rsqrt_fusion, f32[512]{0:T(512)S(1)} %broadcast_multiply_fusion), kind=kOutput, calls=%fused_computation.24 | convolution fusion | flops 1217593344 | bytes 5926912 | tf_op jit(solution)/shard_map/dot_general | solution.py:32
  132.0 0.7 copy-done.5
  132.9 0.7 bitcast_dynamic-update-slice_fusion
  133.7 1.9 multiply_reduce_fusion
  135.6 2.1 copy-done.1
  137.7 0.8 fusion.7
  138.5 6.4 %convolution_convert_fusion = bf16[512,3072]{0,1:T(8,128)(2,1)} fusion(bf16[2048,128]{1,0:T(8,128)(2,1)} %get-tuple-element.15, f32[512,2048]{1,0:T(8,128)} %copy-done.1, f32[512]{0:T(512)S(1)} %fusion.7, f32[512]{0:T(512)S(1)} %get-tuple-element.12, bf16[3072,4,128]{2,0,1:T(8,128)(2,1)} %bitcast.57), kind=kOutput, calls=%fused_computation.11 | convolution fusion | flops 676921344 | bytes 8654848 | tf_op jit(solution)/shard_map/dot_general | solution.py:58
  145.0 194.1 %all-reduce.2.cloned.1.call-done = bf16[512,3072]{0,1:T(8,128)(2,1)} async-done(((bf16[512,3072]{0,1:T(8,128)(2,1)}), bf16[512,3072]{0,1:T(8,128)(2,1)}) %all-reduce.2.cloned.1.call-update) | async-done | bytes 3145744 | tf_op jit(solution)/shard_map/psum | solution.py:61
  339.1 1.1 fusion.22
  340.2 10.4 %collective-permute-start = (bf16[1,512,192]{1,2,0:T(8,128)(2,1)S(1)}, bf16[1,512,192]{1,2,0:T(8,128)(2,1)S(1)}, u32[]{:S(2)}, u32[]{:S(2)}) collective-permute-start(bf16[1,512,192]{1,2,0:T(8,128)(2,1)S(1)} %fusion.22), channel_id=1, source_target_pairs={{496,0},{0,16},{16,32},{32,48},{48,64},{64,80},{80,96},{96,112},{1... | collective-permute-start | bytes 589832 | tf_op jit(solution)/shard_map/ppermute | solution.py:12
  350.6 2.6 collective-permute-done
  (26 shorter events, 1.8 us)
Async XLA Ops:
  6.5 1.9 copy-start
  6.5 107.7 %all-gather.2.cloned.1.call-start = ((), (), s32[]{:S(2)}) async-start(), calls=%async_computation.1 | async-start | bytes 3342336 | tf_op jit(solution)/shard_map/all_gather | solution.py:27
  18.1 14.6 %copy-start.6 = (f32[1,3,3072]{2,0,1:T(1,128)S(1)}, f32[1,3,3072]{2,0,1:T(1,128)}, u32[]{:S(2)}) copy-start(f32[1,3,3072]{2,0,1:T(1,128)} %param.7) | copy-start | bytes 110596
  18.1 99.8 %all-to-all-start = ((bf16[32,96,4,128]{3,2,1,0:T(4,128)(2,1)}), bf16[32,96,4,128]{3,2,1,0:T(4,128)(2,1)}, u32[]{:S(2)}, u32[]{:S(2)}) async-start(bf16[32,96,4,128]{3,2,1,0:T(4,128)(2,1)} %broadcast_select_fusion), calls=%async_computation | async-start | bytes 6291456 | tf_op jit(solution)/shard_map/all_to_all | solution.py:21
  29.5 309.6 %all-reduce.2.cloned.1.call-start = ((), (), s32[]{:S(2)}) async-start(), calls=%async_computation.2 | async-start | bytes 6291456 | tf_op jit(solution)/shard_map/psum | solution.py:61
  114.2 2.8 copy-start.2
  120.3 1.6 copy-start.3
  131.9 0.8 copy-start.5
  135.6 2.1 copy-start.1
  138.5 200.6 %copy-start.4 = (bf16[1,512,192]{1,2,0:T(8,128)(2,1)S(1)}, bf16[1,512,192]{1,2,0:T(8,128)(2,1)}, u32[]{:S(2)}) copy-start(bf16[1,512,192]{1,2,0:T(8,128)(2,1)} %param.8) | copy-start | bytes 589828
  340.2 13.0 %collective-permute-start = (bf16[1,512,192]{1,2,0:T(8,128)(2,1)S(1)}, bf16[1,512,192]{1,2,0:T(8,128)(2,1)S(1)}, u32[]{:S(2)}, u32[]{:S(2)}) collective-permute-start(bf16[1,512,192]{1,2,0:T(8,128)(2,1)S(1)} %fusion.22), channel_id=1, source_target_pairs={{496,0},{0,16},{16,32},{32,48},{48,64},{64,80},{80,96},{96,112},{1... | collective-permute-start | bytes 589832 | tf_op jit(solution)/shard_map/ppermute | solution.py:12
Sparse Core Ops, SparseCore 0:
  10.4 103.7 all-gather.1
  145.0 194.0 all-reduce.1
where the time goes:
time: 362 us; the launch traced here: 361 us
  waiting for transfers between devices  279 us (77%)
  starting transfers between devices  22.1 us (6%)
  local copies, waits for them, and re-layouts  21.8 us (6%)
  between operations  14.2 us (4%)
  matrix products  12.5 us (3%)
  other arithmetic  11.3 us (3%)
    psum x1, waiting for transfers between devices, local(): lax.psum(partial_value.astype(jnp.bfloat16), 'tp').astype(jnp.float32)  194 us
    all_gather x1, waiting for transfers between devices, local(): lax.all_gather(inflow, 'tp', axis=2, tiled=True)[0].astype(jnp.float32)  81.5 us
    all_to_all x1, starting transfers between devices, local(): lax.all_to_all(ordered, 'section', split_axis=0, concat_axis=1, tiled=True)  11.4 us
    ppermute x1, starting transfers between devices, passed_along(): return lax.ppermute(block, axis, route)  10.4 us
  transfers between devices with their start and end apart: 4, of which 3 were waited for; matrix products, arithmetic and copies ran while one was open for 5% of the time, Pallas kernels for 0%

commit v1 on v0

v1 whole, which is shorter than its diff:
```python
import functools

import jax
import jax.numpy as jnp
from jax import lax
from jax.experimental import pallas as pl
from jax.experimental.pallas import tpu as pltpu
from jax.sharding import PartitionSpec as P

MESH = pl.DeviceIdType.MESH
F32 = jnp.float32
BF16 = jnp.bfloat16

HD = 128
D = 3072
PATCH = 512
SEQ = 2048
BLOCKS = 32
N_TP = 16
ROWS = D // BLOCKS
SHARE = D // N_TP
PACKED = PATCH + PATCH // 2
PER_X = D // 4
Q_STEP = 128


def peer_section(k, section):
    core = lax.rem(section, 2)
    y = lax.rem(section // 2, 8)
    z_lo = section // 16
    turn = k // 4
    flip = 3 - lax.rem(k, 4)
    half = (turn + 1) // 2
    dy = 4 + half * (1 - 2 * lax.rem(turn, 2))
    return (lax.rem(z_lo + flip // 2, 2) * 8 + lax.rem(y + dy, 8)) * 2 + lax.rem(core + lax.rem(flip, 2), 2)


def pack(value):
    tail = value[:, HD:SHARE]
    return value[:, :HD], jnp.concatenate([tail[: PATCH // 2], tail[PATCH // 2 :]], axis=1)


def kernel(
    inv_ref, patch_ref, w_hbm, mod_ref, x_hbm, stale_hbm, out_ref,
    w_v, x_v, stale_v, perm_v, send_w, wqkv, wo, xg, normed, q_v, k_v, v_v,
    o_stale, m_stale, l_stale, p_new, m_new, l_new, attg, part, rs_in, own, res, hand,
    sem_loc, ss_w, rs_w, rs_o, ss_own, ss_x, rs_x, ss_f, ss_a, rs_a, ss_r, rs_r, ss_h, rs_h,
):
    section = lax.axis_index("section")
    t = lax.axis_index("tp")
    x = t // 4
    zh = lax.rem(t, 4)
    y = lax.rem(section // 2, 8)
    xo = section // 8

    load_w = pltpu.make_async_copy(w_hbm, w_v, sem_loc.at[0])
    load_x = pltpu.make_async_copy(x_hbm, x_v, sem_loc.at[1])
    load_s = pltpu.make_async_copy(stale_hbm, stale_v, sem_loc.at[2])
    load_x.start()
    load_w.start()
    load_s.start()

    barrier = pltpu.get_barrier_semaphore()

    def greet(dev):
        pl.semaphore_signal(barrier, inc=1, device_id=dev, device_id_type=MESH)

    @pl.loop(0, BLOCKS - 1)
    def _(k):
        greet((peer_section(k, section), t))

    @pl.loop(0, BLOCKS)
    def _(k):
        greet((x * 8 + k // 4, lax.rem(k, 4) * 4 + zh))

    for d in range(1, 4):
        greet((section, lax.rem(x + d, 4) * 4 + zh))
        greet((section, x * 4 + lax.rem(zh + d, 4)))

    row = lax.broadcasted_iota(jnp.int32, (4 * ROWS, 4 * ROWS), 0)
    col = lax.broadcasted_iota(jnp.int32, (4 * ROWS, 4 * ROWS), 1)
    proj = (row >= ROWS).astype(jnp.int32) + (row >= 2 * ROWS).astype(jnp.int32) + (row >= 3 * ROWS).astype(jnp.int32)
    perm_v[...] = jnp.where(col == (row - proj * ROWS) * 4 + proj, 1.0, 0.0).astype(BF16)

    load_x.wait()
    head, tail = pack(x_v[...].astype(F32))
    xg[t, pl.ds(0, PATCH), :] = head.astype(BF16)
    xg[t, pl.ds(PATCH, PATCH // 2), :] = tail.astype(BF16)
    load_w.wait()

    pl.semaphore_wait(barrier, (BLOCKS - 1) + BLOCKS + 6)

    def send_x(slot, dev, sem):
        return pltpu.make_async_remote_copy(
            xg.at[slot], xg.at[slot], sem, rs_x.at[slot], device_id=dev, device_id_type=MESH
        )

    for d in range(1, 4):
        send_x(t, (section, x * 4 + lax.rem(zh + d, 4)), ss_x.at[d - 1]).start()
    for d in range(1, 4):
        send_x(t, (section, lax.rem(x + d, 4) * 4 + zh), ss_x.at[2 + d]).start()

    def sorted_rows(s):
        block = w_v[inv_ref[s]]
        return jnp.dot(perm_v[...], block, preferred_element_type=F32).astype(BF16)

    my_rows = pl.ds(pl.multiple_of(section * ROWS, ROWS), ROWS)

    def send_part(k, p):
        return pltpu.make_async_remote_copy(
            send_w.at[k, pl.ds(p * ROWS, ROWS)], wqkv.at[p, my_rows], ss_w.at[p], rs_w.at[p],
            device_id=(peer_section(k, section), t), device_id_type=MESH,
        )

    o_rows = pl.ds(pl.multiple_of(lax.rem(section, 8) * ROWS, ROWS), ROWS)
    o_group = lax.rem(section // 2, 4)

    def send_o(k, sem):
        return pltpu.make_async_remote_copy(
            send_w.at[k, pl.ds(3 * ROWS, ROWS)], wo.at[x, o_rows], sem, rs_o.at[o_group],
            device_id=(peer_section(k, section), xo * 4 + zh), device_id_type=MESH,
        )

    @pl.loop(0, BLOCKS - 1)
    def _(k):
        send_w[k] = sorted_rows(peer_section(k, section))
        send_part(k, 0).start()

    mine = sorted_rows(section)
    send_w[BLOCKS - 1] = mine
    for p in range(3):
        wqkv[p, my_rows, :] = mine[p * ROWS : (p + 1) * ROWS]

    for p in (1, 2):
        @pl.loop(0, BLOCKS - 1)
        def _(k):
            send_part(k, p).start()

    @pl.loop(0, BLOCKS - 1)
    def _(k):
        send_o(k, ss_w.at[3]).start()

    own_o = pltpu.make_async_copy(
        send_w.at[BLOCKS - 1, pl.ds(3 * ROWS, ROWS)], wo.at[x, o_rows], rs_o.at[o_group]
    )

    @pl.when(xo == x)
    def _():
        own_o.start()

    @pl.when(xo != x)
    def _():
        send_o(BLOCKS - 1, ss_own).start()

    for d in range(1, 4):
        slot = x * 4 + lax.rem(zh + d, 4)
        send_x(slot, (section, slot), ss_x.at[0]).wait_recv()
        for e in range(1, 4):
            dev = (section, lax.rem(x + e, 4) * 4 + zh)
            send_x(slot, dev, ss_f.at[3 * (d - 1) + e - 1]).start()

    for e in range(1, 4):
        for d in range(4):
            slot = lax.rem(x + e, 4) * 4 + lax.rem(zh + d, 4)
            send_x(slot, (section, slot), ss_x.at[0]).wait_recv()

    for h in range(2):
        @pl.loop(0, 8)
        def _(i):
            rows = pl.ds(pl.multiple_of(h * 256 + i * 32, 32), 32)
            tails = pl.ds(pl.multiple_of(PATCH + i * 32, 32), 32)
            pieces = []
            for u in range(N_TP):
                pieces.append(xg[u, rows, :].astype(F32))
                pieces.append(xg[u, tails, :].astype(F32)[:, 64 * h : 64 * h + 64])
            tokens = jnp.concatenate(pieces, axis=1)
            center = jnp.mean(tokens, axis=1, keepdims=True)
            shifted = tokens - center
            spread = jnp.mean(shifted * shifted, axis=1, keepdims=True)
            value = shifted * lax.rsqrt(spread + 1e-06)
            normed[rows, :] = (value * (1.0 + mod_ref[0:1, :]) + mod_ref[1:2, :]).astype(BF16)

    def wait_weights(p):
        view = wqkv.at[p, pl.ds(0, D - ROWS)]
        pltpu.make_async_copy(view, view, rs_w.at[p]).wait()

    def project(p, dst):
        @pl.loop(0, PATCH // Q_STEP)
        def _(i):
            rows = pl.ds(pl.multiple_of(i * Q_STEP, Q_STEP), Q_STEP)
            dst[rows, :] = jnp.dot(normed[rows, :], wqkv[p], preferred_element_type=F32).astype(BF16)

    NT = (((1,), (1,)), ((), ()))
    scaling = HD ** -0.5

    wait_weights(0)
    project(0, q_v)
    load_s.wait()
    patch = patch_ref[0]

    @pl.loop(0, PATCH // Q_STEP)
    def _(i):
        rows = pl.ds(pl.multiple_of(i * Q_STEP, Q_STEP), Q_STEP)
        query = q_v[rows, :]
        scores = []
        for j in range(1, 4):
            keys = stale_v[0, lax.rem(patch + j, 4)]
            scores.append(lax.dot_general(query, keys, NT, preferred_element_type=F32) * scaling)
        scores = jnp.concatenate(scores, axis=1)
        top = jnp.max(scores, axis=1, keepdims=True)
        expo = jnp.exp(scores - top)
        m_stale[rows, :] = jnp.broadcast_to(top, (Q_STEP, HD))
        l_stale[rows, :] = jnp.broadcast_to(jnp.sum(expo, axis=1, keepdims=True), (Q_STEP, HD))
        weights = expo.astype(BF16)
        total = jnp.zeros((Q_STEP, HD), F32)
        for j in range(1, 4):
            values = stale_v[1, lax.rem(patch + j, 4)]
            total += jnp.dot(weights[:, (j - 1) * PATCH : j * PATCH], values, preferred_element_type=F32)
        o_stale[rows, :] = total

    wait_weights(1)
    project(1, k_v)

    @pl.loop(0, PATCH // Q_STEP)
    def _(i):
        rows = pl.ds(pl.multiple_of(i * Q_STEP, Q_STEP), Q_STEP)
        scores = lax.dot_general(q_v[rows, :], k_v[...], NT, preferred_element_type=F32) * scaling
        top = jnp.max(scores, axis=1, keepdims=True)
        expo = jnp.exp(scores - top)
        l_part = jnp.broadcast_to(jnp.sum(expo, axis=1, keepdims=True), (Q_STEP, HD))
        top = jnp.broadcast_to(top, (Q_STEP, HD))
        high = jnp.maximum(top, m_stale[rows, :])
        a_new = jnp.exp(top - high)
        a_old = jnp.exp(m_stale[rows, :] - high)
        inverse = 1.0 / (a_new * l_part + a_old * l_stale[rows, :])
        m_new[rows, :] = a_new * inverse
        o_stale[rows, :] = o_stale[rows, :] * (a_old * inverse)
        p_new[rows, :] = expo.astype(BF16)

    wait_weights(2)
    project(2, v_v)

    @pl.loop(0, PATCH // Q_STEP)
    def _(i):
        rows = pl.ds(pl.multiple_of(i * Q_STEP, Q_STEP), Q_STEP)
        fresh = jnp.dot(p_new[rows, :], v_v[...], preferred_element_type=F32)
        attg[x, rows, :] = (o_stale[rows, :] + fresh * m_new[rows, :]).astype(BF16)

    def send_a(slot, e, sem):
        return pltpu.make_async_remote_copy(
            attg.at[slot], attg.at[slot], sem, rs_a.at[slot],
            device_id=(section, lax.rem(x + e, 4) * 4 + zh), device_id_type=MESH,
        )

    for e in range(1, 4):
        send_a(x, e, ss_a.at[e - 1]).start()
    for e in range(1, 4):
        send_a(lax.rem(x + e, 4), e, ss_a.at[e - 1]).wait_recv()

    def send_r(d):
        return pltpu.make_async_remote_copy(
            part.at[d - 1], rs_in.at[d - 1], ss_r.at[d - 1], rs_r.at[d - 1],
            device_id=(section, x * 4 + lax.rem(zh + d, 4)), device_id_type=MESH,
        )

    attended = jnp.concatenate([attg[i] for i in range(4)], axis=1)
    for d in (2, 1, 3, 0):
        group = lax.rem(zh + d, 4)
        features = pl.ds(pl.multiple_of(group * SHARE, SHARE), SHARE)
        view = wqkv.at[0, pl.ds(0, 8 * ROWS)]
        pltpu.make_async_copy(view, view, rs_o.at[group]).wait()
        weights = jnp.concatenate([wo[i, features, :] for i in range(4)], axis=1)
        partial_g = lax.dot_general(attended, weights, NT, preferred_element_type=F32)
        head, tail = pack(partial_g)
        if d > 0:
            part[d - 1, pl.ds(0, PATCH), :] = head.astype(BF16)
            part[d - 1, pl.ds(PATCH, PATCH // 2), :] = tail.astype(BF16)
            send_r(d).start()
        else:
            own[pl.ds(0, PATCH), :] = head
            own[pl.ds(PATCH, PATCH // 2), :] = tail

    gate = jnp.zeros((1, SHARE), F32)
    for u in range(N_TP):
        gate = jnp.where(t == u, mod_ref[2:3, u * SHARE : (u + 1) * SHARE], gate)
    gate_head = gate[:, :HD]
    gate_tail = jnp.concatenate([gate[:, HD:], gate[:, HD:]], axis=1)

    for d in (1, 2, 3):
        send_r(d).wait_recv()
    for start, size, g in ((0, PATCH, gate_head), (PATCH, PATCH // 2, gate_tail)):
        rows = pl.ds(start, size)
        mixed = own[rows, :] + rs_in[0, rows, :].astype(F32)
        mixed = mixed + rs_in[1, rows, :].astype(F32) + rs_in[2, rows, :].astype(F32)
        res[rows, :] = (xg[t, rows, :].astype(F32) + g * mixed).astype(BF16)

    handed = pltpu.make_async_remote_copy(
        res, hand, ss_h, rs_h, device_id=(lax.rem(section + 1, BLOCKS), t), device_id_type=MESH
    )
    handed.start()

    for p in range(4):
        view = wqkv.at[0, pl.ds(0, D - ROWS)]
        pltpu.make_async_copy(view, view, ss_w.at[p]).wait()

    @pl.when(xo != x)
    def _():
        send_o(BLOCKS - 1, ss_own).wait_send()

    for d in range(6):
        send_x(t, (section, t), ss_x.at[d]).wait_send()
    for d in range(9):
        send_x(t, (section, t), ss_f.at[d]).wait_send()
    for d in range(3):
        send_a(x, d + 1, ss_a.at[d]).wait_send()
        send_r(d + 1).wait_send()

    handed.wait()
    final_head = hand[pl.ds(0, PATCH), :].astype(F32)
    final_tail = hand[pl.ds(PATCH, PATCH // 2), :].astype(F32)
    final_tail = jnp.concatenate([final_tail[:, :64], final_tail[:, 64:]], axis=0)
    out_ref[...] = jnp.concatenate([final_head, final_tail], axis=1).astype(BF16)


def local(block_weights, modulation, inflow, stale_cache, patch_index, assignment):
    section_ids = jnp.arange(BLOCKS, dtype=jnp.int32)
    owner_table = (assignment[None, :] == section_ids[:, None]).astype(jnp.int32)
    inverse = jnp.sum(owner_table * section_ids[None, :], axis=1)

    vmem = pl.BlockSpec(memory_space=pltpu.VMEM)
    smem = pl.BlockSpec(memory_space=pltpu.SMEM)
    hbm = pl.BlockSpec(memory_space=pl.ANY)
    dma = pltpu.SemaphoreType.DMA
    result = pl.pallas_call(
        kernel,
        out_shape=jax.ShapeDtypeStruct((PATCH, SHARE), BF16),
        in_specs=[smem, smem, hbm, vmem, hbm, hbm],
        out_specs=vmem,
        scratch_shapes=[
            pltpu.VMEM((BLOCKS, 4 * ROWS, HD), BF16),
            pltpu.VMEM((PATCH, SHARE), BF16),
            pltpu.VMEM((2, 4, PATCH, HD), BF16),
            pltpu.VMEM((4 * ROWS, 4 * ROWS), BF16),
            pltpu.VMEM((BLOCKS, 4 * ROWS, HD), BF16),
            pltpu.VMEM((3, D, HD), BF16),
            pltpu.VMEM((4, PER_X, HD), BF16),
            pltpu.VMEM((N_TP, PACKED, HD), BF16),
            pltpu.VMEM((PATCH, D), BF16),
            pltpu.VMEM((PATCH, HD), BF16),
            pltpu.VMEM((PATCH, HD), BF16),
            pltpu.VMEM((PATCH, HD), BF16),
            pltpu.VMEM((PATCH, HD), F32),
            pltpu.VMEM((PATCH, HD), F32),
            pltpu.VMEM((PATCH, HD), F32),
            pltpu.VMEM((PATCH, PATCH), BF16),
            pltpu.VMEM((PATCH, HD), F32),
            pltpu.VMEM((PATCH, HD), F32),
            pltpu.VMEM((4, PATCH, HD), BF16),
            pltpu.VMEM((3, PACKED, HD), BF16),
            pltpu.VMEM((3, PACKED, HD), BF16),
            pltpu.VMEM((PACKED, HD), F32),
            pltpu.VMEM((PACKED, HD), BF16),
            pltpu.VMEM((PACKED, HD), BF16),
            dma((3,)), dma((4,)), dma((3,)), dma((4,)), dma,
            dma((6,)), dma((N_TP,)), dma((9,)), dma((3,)), dma((4,)), dma((3,)), dma((3,)), dma, dma,
        ],
        compiler_params=pltpu.CompilerParams(
            collective_id=0, has_side_effects=True, vmem_limit_bytes=48 * 2**20
        ),
    )(
        inverse,
        patch_index,
        block_weights.reshape(BLOCKS, 4 * ROWS, HD),
        modulation.reshape(3, D),
        inflow.reshape(PATCH, SHARE),
        stale_cache.reshape(2, 4, PATCH, HD),
    )
    return result[None]


def solution(mesh):
    placed = (
        P(None, "section", None, "tp"),
        P("section", None, None),
        P("section", None, "tp"),
        P("section", None, None, "tp"),
        P("section"),
        P(),
    )
    return jax.shard_map(
        local, mesh=mesh, in_specs=placed, out_specs=P("section", None, "tp"), check_vma=False
    )
```

time: 362 us -> 125 us (0.35)
  the two profiles are of different devices: /device:TPU:1 before, /device:TPU:4 now
where the time goes in v1:
time: 125 us
  Pallas kernels  118 us (94%)
  local copies, waits for them, and re-layouts  5.76 us (5%)
    pallas_call x1, Pallas kernels, local(): pl.pallas_call(kernel, out_shape=jax.ShapeDtypeStruct((PATCH, SHARE), BF1...  118 us
    unnamed x6, local copies, waits for them, and re-layouts  4.96 us

profile of v1, /device:TPU:4, one launch (start us, length us, event | category | flops | bytes accessed | tf_op | source)
XLA Modules:
  0.0 124.9 jit_solution(12115309081441030859)
XLA Ops:
  0.7 0.8 select_reduce_fusion.inv_ref
  1.4 0.8 copy.13
  2.2 1.1 copy.9
  3.3 0.0 copy-start
  3.3 1.9 %copy-done = bf16[32,96,4,128]{3,2,1,0:T(4,128)(2,1)S(1)} copy-done((bf16[32,96,4,128]{3,2,1,0:T(4,128)(2,1)S(1)}, bf16[32,96,4,128]{3,2,1,0:T(4,128)(2,1)}, u32[]{:S(2)}) %copy-start) | copy-done | bytes 3145752
  5.2 0.0 copy-start.1
  5.2 1.2 copy-done.1
  6.4 117.7 %shard_map.64 = bf16[512,192]{1,0:T(8,128)(2,1)S(1)} custom-call(s32[32]{0:T(128)S(1)} %select_reduce_fusion.inv_ref, s32[1]{0:T(128)S(6)} %copy.14.patch_ref, bf16[32,384,128]{2,1,0:T(8,128)(2,1)S(1)} %bitcast.7, f32[3,3072]{1,0:T(4,128)S(1)} %bitcast.11, bf16[512,192]{1,0:T(8,128)(2,1)S(1)} %bitcast.10, bf16[2,4,512,128]{3,2,1,0:T(8,128)(2,1)S(1)} %bitcast.8), custom_call_target="tpu_custom_call" | custom-call | tf_op jit(solution)/shard_map/pallas_call | solution.py:334
  124.1 0.8 copy.10
Async XLA Ops:
  3.3 1.9 %copy-start = (bf16[32,96,4,128]{3,2,1,0:T(4,128)(2,1)S(1)}, bf16[32,96,4,128]{3,2,1,0:T(4,128)(2,1)}, u32[]{:S(2)}) copy-start(bf16[32,96,4,128]{3,2,1,0:T(4,128)(2,1)} %param.6) | copy-start | bytes 9437188
  5.2 1.2 copy-start.1

commit v2 on v1

--- a/solution.py
+++ b/solution.py
@@ -19,7 +19,7 @@
 N_TP = 16
 ROWS = D // BLOCKS
 SHARE = D // N_TP
-PACKED = PATCH + PATCH // 2
+HALF = SHARE // 2
 PER_X = D // 4
 Q_STEP = 128
 
@@ -35,15 +35,10 @@
     return (lax.rem(z_lo + flip // 2, 2) * 8 + lax.rem(y + dy, 8)) * 2 + lax.rem(core + lax.rem(flip, 2), 2)
 
 
-def pack(value):
-    tail = value[:, HD:SHARE]
-    return value[:, :HD], jnp.concatenate([tail[: PATCH // 2], tail[PATCH // 2 :]], axis=1)
-
-
 def kernel(
-    inv_ref, patch_ref, w_hbm, mod_ref, x_hbm, stale_hbm, out_ref,
-    w_v, x_v, stale_v, perm_v, send_w, wqkv, wo, xg, normed, q_v, k_v, v_v,
-    o_stale, m_stale, l_stale, p_new, m_new, l_new, attg, part, rs_in, own, res, hand,
+    assign_ref, patch_ref, w_hbm, mod_hbm, x_hbm, stale_hbm, out_ref,
+    w_v, mod_v, columns, stale_v, perm_v, send_w, wqkv, wo, xg, normed, q_v, k_v, v_v,
+    o_stale, m_stale, l_stale, p_new, m_new, attg, stats, norm_v, quarters, part, far_in, near_in, res,
     sem_loc, ss_w, rs_w, rs_o, ss_own, ss_x, rs_x, ss_f, ss_a, rs_a, ss_r, rs_r, ss_h, rs_h,
 ):
     section = lax.axis_index("section")
@@ -54,10 +49,13 @@
     xo = section // 8
 
     load_w = pltpu.make_async_copy(w_hbm, w_v, sem_loc.at[0])
-    load_x = pltpu.make_async_copy(x_hbm, x_v, sem_loc.at[1])
+    my_features = pl.ds(pl.multiple_of(t * SHARE, SHARE), SHARE)
+    load_x = pltpu.make_async_copy(x_hbm, xg.at[my_features], sem_loc.at[1])
     load_s = pltpu.make_async_copy(stale_hbm, stale_v, sem_loc.at[2])
+    load_m = pltpu.make_async_copy(mod_hbm, mod_v, sem_loc.at[3])
     load_x.start()
     load_w.start()
+    load_m.start()
     load_s.start()
 
     barrier = pltpu.get_barrier_semaphore()
@@ -83,16 +81,14 @@
     perm_v[...] = jnp.where(col == (row - proj * ROWS) * 4 + proj, 1.0, 0.0).astype(BF16)
 
     load_x.wait()
-    head, tail = pack(x_v[...].astype(F32))
-    xg[t, pl.ds(0, PATCH), :] = head.astype(BF16)
-    xg[t, pl.ds(PATCH, PATCH // 2), :] = tail.astype(BF16)
     load_w.wait()
 
     pl.semaphore_wait(barrier, (BLOCKS - 1) + BLOCKS + 6)
 
     def send_x(slot, dev, sem):
-        return pltpu.make_async_remote_copy(
-            xg.at[slot], xg.at[slot], sem, rs_x.at[slot], device_id=dev, device_id_type=MESH
+        rows = pl.ds(pl.multiple_of(slot * SHARE, SHARE), SHARE)
+        return pltpu.make_async_remote_copy(
+            xg.at[rows], xg.at[rows], sem, rs_x.at[slot], device_id=dev, device_id_type=MESH
         )
 
     for d in range(1, 4):
@@ -101,7 +97,10 @@
         send_x(t, (section, lax.rem(x + d, 4) * 4 + zh), ss_x.at[2 + d]).start()
 
     def sorted_rows(s):
-        block = w_v[inv_ref[s]]
+        owner = jnp.int32(0)
+        for b in range(1, BLOCKS):
+            owner = jnp.where(assign_ref[b] == s, b, owner)
+        block = w_v[owner]
         return jnp.dot(perm_v[...], block, preferred_element_type=F32).astype(BF16)
 
     my_rows = pl.ds(pl.multiple_of(section * ROWS, ROWS), ROWS)
@@ -152,33 +151,58 @@
     def _():
         send_o(BLOCKS - 1, ss_own).start()
 
-    for d in range(1, 4):
+    load_m.wait()
+
+    @pl.loop(0, D // HD)
+    def _(c):
+        features = pl.ds(pl.multiple_of(c * HD, HD), HD)
+        for p in range(3):
+            columns[p, features, :] = jnp.broadcast_to(mod_v[p, :, features], (HD, HD)).T
+
+    def take_stats(slot):
+        rows = pl.ds(pl.multiple_of(slot * SHARE, SHARE), SHARE)
+        tokens = xg[rows, :].astype(F32)
+        mean = jnp.sum(jnp.sum(tokens.reshape(SHARE // 8, 8, PATCH), axis=0), axis=0, keepdims=True) / SHARE
+        shifted = tokens - mean
+        shifted = shifted * shifted
+        moment = jnp.sum(jnp.sum(shifted.reshape(SHARE // 8, 8, PATCH), axis=0), axis=0, keepdims=True)
+        stats[slot] = jnp.concatenate([mean, moment], axis=0)
+
+    @pl.loop(1, 4)
+    def _(d):
         slot = x * 4 + lax.rem(zh + d, 4)
         send_x(slot, (section, slot), ss_x.at[0]).wait_recv()
         for e in range(1, 4):
             dev = (section, lax.rem(x + e, 4) * 4 + zh)
             send_x(slot, dev, ss_f.at[3 * (d - 1) + e - 1]).start()
 
-    for e in range(1, 4):
-        for d in range(4):
-            slot = lax.rem(x + e, 4) * 4 + lax.rem(zh + d, 4)
-            send_x(slot, (section, slot), ss_x.at[0]).wait_recv()
-
-    for h in range(2):
-        @pl.loop(0, 8)
-        def _(i):
-            rows = pl.ds(pl.multiple_of(h * 256 + i * 32, 32), 32)
-            tails = pl.ds(pl.multiple_of(PATCH + i * 32, 32), 32)
-            pieces = []
-            for u in range(N_TP):
-                pieces.append(xg[u, rows, :].astype(F32))
-                pieces.append(xg[u, tails, :].astype(F32)[:, 64 * h : 64 * h + 64])
-            tokens = jnp.concatenate(pieces, axis=1)
-            center = jnp.mean(tokens, axis=1, keepdims=True)
-            shifted = tokens - center
-            spread = jnp.mean(shifted * shifted, axis=1, keepdims=True)
-            value = shifted * lax.rsqrt(spread + 1e-06)
-            normed[rows, :] = (value * (1.0 + mod_ref[0:1, :]) + mod_ref[1:2, :]).astype(BF16)
+    @pl.loop(0, 4)
+    def _(d):
+        take_stats(x * 4 + lax.rem(zh + d, 4))
+
+    @pl.loop(0, 12)
+    def _(i):
+        slot = lax.rem(x + 1 + lax.rem(i, 3), 4) * 4 + lax.rem(zh + i // 3, 4)
+        send_x(slot, (section, slot), ss_x.at[0]).wait_recv()
+        take_stats(slot)
+
+    means = stats[:, 0, :]
+    center = jnp.sum(means, axis=0, keepdims=True) / N_TP
+    means = means - center
+    moment = jnp.sum(stats[:, 1, :] + SHARE * means * means, axis=0, keepdims=True)
+    inverse = lax.rsqrt(moment / D + 1e-06)
+    norm_v[0:1, :] = center
+    norm_v[1:2, :] = inverse
+
+    @pl.loop(0, D // HD)
+    def _(c):
+        features = pl.ds(pl.multiple_of(c * HD, HD), HD)
+        scale = 1.0 + columns[0, features, :]
+        shift = columns[1, features, :]
+        for i in range(PATCH // HD):
+            tokens = pl.ds(i * HD, HD)
+            value = (xg[features, tokens].astype(F32) - norm_v[0:1, tokens]) * norm_v[1:2, tokens]
+            normed[tokens, features] = (value * scale + shift).T.astype(BF16)
 
     def wait_weights(p):
         view = wqkv.at[p, pl.ds(0, D - ROWS)]
@@ -257,47 +281,82 @@
     for e in range(1, 4):
         send_a(lax.rem(x + e, 4), e, ss_a.at[e - 1]).wait_recv()
 
-    def send_r(d):
-        return pltpu.make_async_remote_copy(
-            part.at[d - 1], rs_in.at[d - 1], ss_r.at[d - 1], rs_r.at[d - 1],
-            device_id=(section, x * 4 + lax.rem(zh + d, 4)), device_id_type=MESH,
-        )
-
-    attended = jnp.concatenate([attg[i] for i in range(4)], axis=1)
-    for d in (2, 1, 3, 0):
-        group = lax.rem(zh + d, 4)
+    def along(sign):
+        return (section, x * 4 + lax.rem(zh + 4 + sign, 4))
+
+    def remote(src, dst, k, sign):
+        return pltpu.make_async_remote_copy(
+            src, dst, ss_r.at[k], rs_r.at[k], device_id=along(sign), device_id_type=MESH
+        )
+
+    low, high = pl.ds(0, HALF), pl.ds(HALF, HALF)
+    far_up = remote(part.at[0, low], far_in.at[0], 0, 1)
+    far_down = remote(part.at[0, high], far_in.at[1], 1, -1)
+    plain_up = remote(part.at[1, high], near_in.at[0, high], 2, 1)
+    plain_down = remote(part.at[2, low], near_in.at[1, low], 3, -1)
+    sum_up = remote(part.at[1, low], near_in.at[0, low], 4, 1)
+    sum_down = remote(part.at[2, high], near_in.at[1, high], 5, -1)
+
+    at = lax.rem(y, 4)
+    rising = 228 - 3 * at - 84 * at * (at - 1) + 52 * at * (at - 1) * (at - 2)
+    falling = 27 + 48 * at + 33 * ((at * (at - 1)) // 2) - 7 * at * (at - 1) * (at - 2)
+    other = lax.rem(y // 4 + lax.rem(x, 2), 2)
+
+    def quarter(i, code):
+        group = lax.rem(code, 4)
+        step = lax.rem(group - zh + 4, 4)
         features = pl.ds(pl.multiple_of(group * SHARE, SHARE), SHARE)
         view = wqkv.at[0, pl.ds(0, 8 * ROWS)]
         pltpu.make_async_copy(view, view, rs_o.at[group]).wait()
-        weights = jnp.concatenate([wo[i, features, :] for i in range(4)], axis=1)
-        partial_g = lax.dot_general(attended, weights, NT, preferred_element_type=F32)
-        head, tail = pack(partial_g)
-        if d > 0:
-            part[d - 1, pl.ds(0, PATCH), :] = head.astype(BF16)
-            part[d - 1, pl.ds(PATCH, PATCH // 2), :] = tail.astype(BF16)
-            send_r(d).start()
-        else:
-            own[pl.ds(0, PATCH), :] = head
-            own[pl.ds(PATCH, PATCH // 2), :] = tail
-
-    gate = jnp.zeros((1, SHARE), F32)
-    for u in range(N_TP):
-        gate = jnp.where(t == u, mod_ref[2:3, u * SHARE : (u + 1) * SHARE], gate)
-    gate_head = gate[:, :HD]
-    gate_tail = jnp.concatenate([gate[:, HD:], gate[:, HD:]], axis=1)
-
-    for d in (1, 2, 3):
-        send_r(d).wait_recv()
-    for start, size, g in ((0, PATCH, gate_head), (PATCH, PATCH // 2, gate_tail)):
-        rows = pl.ds(start, size)
-        mixed = own[rows, :] + rs_in[0, rows, :].astype(F32)
-        mixed = mixed + rs_in[1, rows, :].astype(F32) + rs_in[2, rows, :].astype(F32)
-        res[rows, :] = (xg[t, rows, :].astype(F32) + g * mixed).astype(BF16)
-
-    handed = pltpu.make_async_remote_copy(
-        res, hand, ss_h, rs_h, device_id=(lax.rem(section + 1, BLOCKS), t), device_id_type=MESH
-    )
-    handed.start()
+        attended = jnp.concatenate([attg[j] for j in range(4)], axis=1)
+        weights = jnp.concatenate([wo[j, features, :] for j in range(4)], axis=1)
+        quarters[step] = lax.dot_general(weights, attended, NT, preferred_element_type=F32)
+
+        @pl.when(step == 2)
+        def _():
+            part[0] = quarters[2].astype(BF16)
+            far_up.start()
+            far_down.start()
+
+        @pl.when(step == 1)
+        def _():
+            part[1, high, :] = quarters[1, high, :].astype(BF16)
+            plain_up.start()
+
+        @pl.when(step == 3)
+        def _():
+            part[2, low, :] = quarters[3, low, :].astype(BF16)
+            plain_down.start()
+
+        return code // 4
+
+    lax.fori_loop(0, 4, quarter, other * rising + (1 - other) * falling)
+
+    far_up.wait_recv()
+    part[1, low, :] = (quarters[1, low, :] + far_in[0].astype(F32)).astype(BF16)
+    sum_up.start()
+    far_down.wait_recv()
+    part[2, high, :] = (quarters[3, high, :] + far_in[1].astype(F32)).astype(BF16)
+    sum_down.start()
+
+    def hand(k):
+        rows = pl.ds(k * HALF, HALF)
+        return pltpu.make_async_remote_copy(
+            res.at[rows], out_ref.at[rows], ss_h.at[k], rs_h.at[k],
+            device_id=(lax.rem(section + 1, BLOCKS), t), device_id_type=MESH,
+        )
+
+    for k, first, second in ((0, plain_down, sum_up), (1, plain_up, sum_down)):
+        first.wait_recv()
+        second.wait_recv()
+        rows = pl.ds(k * HALF, HALF)
+        mine_rows = pl.ds(pl.multiple_of(t * SHARE + k * HALF, HALF), HALF)
+        gate = columns[2, mine_rows, :]
+        for i in range(PATCH // HD):
+            tokens = pl.ds(i * HD, HD)
+            mixed = quarters[0, rows, tokens] + near_in[0, rows, tokens].astype(F32) + near_in[1, rows, tokens].astype(F32)
+            res[rows, tokens] = (xg[mine_rows, tokens].astype(F32) + gate * mixed).astype(BF16)
+        hand(k).start()
 
     for p in range(4):
         view = wqkv.at[0, pl.ds(0, D - ROWS)]
@@ -313,38 +372,32 @@
         send_x(t, (section, t), ss_f.at[d]).wait_send()
     for d in range(3):
         send_a(x, d + 1, ss_a.at[d]).wait_send()
-        send_r(d + 1).wait_send()
-
-    handed.wait()
-    final_head = hand[pl.ds(0, PATCH), :].astype(F32)
-    final_tail = hand[pl.ds(PATCH, PATCH // 2), :].astype(F32)
-    final_tail = jnp.concatenate([final_tail[:, :64], final_tail[:, 64:]], axis=0)
-    out_ref[...] = jnp.concatenate([final_head, final_tail], axis=1).astype(BF16)
+    for copy in (far_up, far_down, plain_up, plain_down, sum_up, sum_down):
+        copy.wait_send()
+    for k in range(2):
+        hand(k).wait()
 
 
 def local(block_weights, modulation, inflow, stale_cache, patch_index, assignment):
-    section_ids = jnp.arange(BLOCKS, dtype=jnp.int32)
-    owner_table = (assignment[None, :] == section_ids[:, None]).astype(jnp.int32)
-    inverse = jnp.sum(owner_table * section_ids[None, :], axis=1)
-
     vmem = pl.BlockSpec(memory_space=pltpu.VMEM)
     smem = pl.BlockSpec(memory_space=pltpu.SMEM)
-    hbm = pl.BlockSpec(memory_space=pl.ANY)
+    hbm = pl.BlockSpec(memory_space=pltpu.HBM)
     dma = pltpu.SemaphoreType.DMA
     result = pl.pallas_call(
         kernel,
-        out_shape=jax.ShapeDtypeStruct((PATCH, SHARE), BF16),
-        in_specs=[smem, smem, hbm, vmem, hbm, hbm],
+        out_shape=jax.ShapeDtypeStruct((SHARE, PATCH), BF16),
+        in_specs=[smem, smem, hbm, hbm, hbm, hbm],
         out_specs=vmem,
         scratch_shapes=[
             pltpu.VMEM((BLOCKS, 4 * ROWS, HD), BF16),
-            pltpu.VMEM((PATCH, SHARE), BF16),
+            pltpu.VMEM((3, 1, D), F32),
+            pltpu.VMEM((3, D, HD), F32),
             pltpu.VMEM((2, 4, PATCH, HD), BF16),
             pltpu.VMEM((4 * ROWS, 4 * ROWS), BF16),
             pltpu.VMEM((BLOCKS, 4 * ROWS, HD), BF16),
             pltpu.VMEM((3, D, HD), BF16),
             pltpu.VMEM((4, PER_X, HD), BF16),
-            pltpu.VMEM((N_TP, PACKED, HD), BF16),
+            pltpu.VMEM((D, PATCH), BF16),
             pltpu.VMEM((PATCH, D), BF16),
             pltpu.VMEM((PATCH, HD), BF16),
             pltpu.VMEM((PATCH, HD), BF16),
@@ -354,28 +407,29 @@
             pltpu.VMEM((PATCH, HD), F32),
             pltpu.VMEM((PATCH, PATCH), BF16),
             pltpu.VMEM((PATCH, HD), F32),
-            pltpu.VMEM((PATCH, HD), F32),
             pltpu.VMEM((4, PATCH, HD), BF16),
-            pltpu.VMEM((3, PACKED, HD), BF16),
-            pltpu.VMEM((3, PACKED, HD), BF16),
-            pltpu.VMEM((PACKED, HD), F32),
-            pltpu.VMEM((PACKED, HD), BF16),
-            pltpu.VMEM((PACKED, HD), BF16),
-            dma((3,)), dma((4,)), dma((3,)), dma((4,)), dma,
-            dma((6,)), dma((N_TP,)), dma((9,)), dma((3,)), dma((4,)), dma((3,)), dma((3,)), dma, dma,
+            pltpu.VMEM((N_TP, 2, PATCH), F32),
+            pltpu.VMEM((8, PATCH), F32),
+            pltpu.VMEM((4, SHARE, PATCH), F32),
+            pltpu.VMEM((3, SHARE, PATCH), BF16),
+            pltpu.VMEM((2, HALF, PATCH), BF16),
+            pltpu.VMEM((2, SHARE, PATCH), BF16),
+            pltpu.VMEM((SHARE, PATCH), BF16),
+            dma((4,)), dma((4,)), dma((3,)), dma((4,)), dma,
+            dma((6,)), dma((N_TP,)), dma((9,)), dma((3,)), dma((4,)), dma((6,)), dma((6,)), dma((2,)), dma((2,)),
         ],
         compiler_params=pltpu.CompilerParams(
-            collective_id=0, has_side_effects=True, vmem_limit_bytes=48 * 2**20
+            collective_id=0, has_side_effects=True, vmem_limit_bytes=60 * 2**20
         ),
     )(
-        inverse,
+        assignment,
         patch_index,
         block_weights.reshape(BLOCKS, 4 * ROWS, HD),
-        modulation.reshape(3, D),
-        inflow.reshape(PATCH, SHARE),
+        modulation.transpose(1, 0, 2),
+        inflow[0].T,
         stale_cache.reshape(2, 4, PATCH, HD),
     )
-    return result[None]
+    return result.T[None]
 
 
 def solution(mesh):

time: 125 us -> 116 us (0.928)
  the two profiles are of different devices: /device:TPU:4 before, /device:TPU:1 now
where the time goes in v2:
time: 116 us; the launch traced here: 115 us
  Pallas kernels  113 us (97%)
  local copies, waits for them, and re-layouts  1.62 us (1%)
    pallas_call x1, Pallas kernels, local(): pl.pallas_call(kernel, out_shape=jax.ShapeDtypeStruct((SHARE, PATCH), BF1...  113 us

profile of v2, /device:TPU:1, one launch (start us, length us, event | category | flops | bytes accessed | tf_op | source)
XLA Modules:
  0.0 115.4 jit_solution(13727709435153110408)
XLA Ops:
  0.7 113.2 %shard_map.64 = bf16[192,512]{1,0:T(8,128)(2,1)} custom-call(s32[32]{0:T(128)} %assign_ref.1, s32[1]{0:T(128)S(6)} %copy.8.patch_ref, bf16[32,384,128]{2,1,0:T(8,128)(2,1)} %bitcast.9, f32[3,1,3072]{2,1,0:T(1,128)} %bitcast.13, bf16[192,512]{1,0:T(8,128)(2,1)} %bitcast.12, bf16[2,4,512,128]{3,2,1,0:T(8,128)(2,1)} %bitcast.10), custom_call_target="tpu_custom_call" | custom-call | tf_op jit(solution)/shard_map/pallas_call | solution.py:386
  113.8 1.6 %copy.9 = bf16[1,512,192]{1,2,0:T(8,128)(2,1)} copy(bf16[1,512,192]{1,2,0:T(8,128)(2,1)} %bitcast.11) | data formatting | bytes 393216

commit v3 on v2

--- a/solution.py
+++ b/solution.py
@@ -20,6 +20,7 @@
 ROWS = D // BLOCKS
 SHARE = D // N_TP
 HALF = SHARE // 2
+CHUNKS = PATCH // HD
 PER_X = D // 4
 Q_STEP = 128
 
@@ -91,17 +92,27 @@
             xg.at[rows], xg.at[rows], sem, rs_x.at[slot], device_id=dev, device_id_type=MESH
         )
 
-    for d in range(1, 4):
-        send_x(t, (section, x * 4 + lax.rem(zh + d, 4)), ss_x.at[d - 1]).start()
+    def send_z(d):
+        return send_x(t, (section, x * 4 + lax.rem(zh + d, 4)), ss_x.at[d - 1])
+
+    def pass_on(d):
+        slot = x * 4 + lax.rem(zh + d, 4)
+        send_x(slot, (section, slot), ss_x.at[0]).wait_recv()
+        for e in range(1, 4):
+            dev = (section, lax.rem(x + e, 4) * 4 + zh)
+            send_x(slot, dev, ss_f.at[3 * (d - 1) + e - 1]).start()
+
+    send_z(1).start()
+    send_z(3).start()
+    send_z(2).start()
     for d in range(1, 4):
         send_x(t, (section, lax.rem(x + d, 4) * 4 + zh), ss_x.at[2 + d]).start()
 
-    def sorted_rows(s):
+    def block_of(s):
         owner = jnp.int32(0)
         for b in range(1, BLOCKS):
             owner = jnp.where(assign_ref[b] == s, b, owner)
-        block = w_v[owner]
-        return jnp.dot(perm_v[...], block, preferred_element_type=F32).astype(BF16)
+        return w_v[owner]
 
     my_rows = pl.ds(pl.multiple_of(section * ROWS, ROWS), ROWS)
 
@@ -120,20 +131,33 @@
             device_id=(peer_section(k, section), xo * 4 + zh), device_id_type=MESH,
         )
 
+    @pl.loop(0, BLOCKS // 4)
+    def _(g):
+        blocks = jnp.concatenate([block_of(peer_section(4 * g + i, section)) for i in range(4)], axis=1)
+        ordered = jnp.dot(perm_v[...], blocks, preferred_element_type=F32).astype(BF16)
+        for i in range(4):
+            send_w[4 * g + i] = ordered[:, i * HD : (i + 1) * HD]
+        for i in range(3):
+            send_part(4 * g + i, 0).start()
+
+        @pl.when(g < BLOCKS // 4 - 1)
+        def _():
+            send_part(4 * g + 3, 0).start()
+
+    for p in range(3):
+        wqkv[p, my_rows, :] = send_w[BLOCKS - 1, pl.ds(p * ROWS, ROWS), :]
+    pass_on(1)
+    pass_on(3)
+
     @pl.loop(0, BLOCKS - 1)
     def _(k):
-        send_w[k] = sorted_rows(peer_section(k, section))
-        send_part(k, 0).start()
-
-    mine = sorted_rows(section)
-    send_w[BLOCKS - 1] = mine
-    for p in range(3):
-        wqkv[p, my_rows, :] = mine[p * ROWS : (p + 1) * ROWS]
-
-    for p in (1, 2):
-        @pl.loop(0, BLOCKS - 1)
-        def _(k):
-            send_part(k, p).start()
+        send_part(k, 1).start()
+
+    pass_on(2)
+
+    @pl.loop(0, BLOCKS - 1)
+    def _(k):
+        send_part(k, 2).start()
 
     @pl.loop(0, BLOCKS - 1)
     def _(k):
@@ -167,14 +191,6 @@
         shifted = shifted * shifted
         moment = jnp.sum(jnp.sum(shifted.reshape(SHARE // 8, 8, PATCH), axis=0), axis=0, keepdims=True)
         stats[slot] = jnp.concatenate([mean, moment], axis=0)
-
-    @pl.loop(1, 4)
-    def _(d):
-        slot = x * 4 + lax.rem(zh + d, 4)
-        send_x(slot, (section, slot), ss_x.at[0]).wait_recv()
-        for e in range(1, 4):
-            dev = (section, lax.rem(x + e, 4) * 4 + zh)
-            send_x(slot, dev, ss_f.at[3 * (d - 1) + e - 1]).start()
 
     @pl.loop(0, 4)
     def _(d):
@@ -284,18 +300,30 @@
     def along(sign):
         return (section, x * 4 + lax.rem(zh + 4 + sign, 4))
 
-    def remote(src, dst, k, sign):
-        return pltpu.make_async_remote_copy(
-            src, dst, ss_r.at[k], rs_r.at[k], device_id=along(sign), device_id_type=MESH
+    def remote(src, dst, k, c, sign):
+        return pltpu.make_async_remote_copy(
+            src, dst, ss_r.at[k, c], rs_r.at[k, c], device_id=along(sign), device_id_type=MESH
         )
 
     low, high = pl.ds(0, HALF), pl.ds(HALF, HALF)
-    far_up = remote(part.at[0, low], far_in.at[0], 0, 1)
-    far_down = remote(part.at[0, high], far_in.at[1], 1, -1)
-    plain_up = remote(part.at[1, high], near_in.at[0, high], 2, 1)
-    plain_down = remote(part.at[2, low], near_in.at[1, low], 3, -1)
-    sum_up = remote(part.at[1, low], near_in.at[0, low], 4, 1)
-    sum_down = remote(part.at[2, high], near_in.at[1, high], 5, -1)
+
+    def far_up(c):
+        return remote(part.at[0, c, low], far_in.at[0, c], 0, c, 1)
+
+    def far_down(c):
+        return remote(part.at[0, c, high], far_in.at[1, c], 1, c, -1)
+
+    def plain_up(c):
+        return remote(part.at[1, c, high], near_in.at[0, c, high], 2, c, 1)
+
+    def plain_down(c):
+        return remote(part.at[2, c, low], near_in.at[1, c, low], 3, c, -1)
+
+    def sum_up(c):
+        return remote(part.at[1, c, low], near_in.at[0, c, low], 4, c, 1)
+
+    def sum_down(c):
+        return remote(part.at[2, c, high], near_in.at[1, c, high], 5, c, -1)
 
     at = lax.rem(y, 4)
     rising = 228 - 3 * at - 84 * at * (at - 1) + 52 * at * (at - 1) * (at - 2)
@@ -308,55 +336,59 @@
         features = pl.ds(pl.multiple_of(group * SHARE, SHARE), SHARE)
         view = wqkv.at[0, pl.ds(0, 8 * ROWS)]
         pltpu.make_async_copy(view, view, rs_o.at[group]).wait()
-        attended = jnp.concatenate([attg[j] for j in range(4)], axis=1)
         weights = jnp.concatenate([wo[j, features, :] for j in range(4)], axis=1)
-        quarters[step] = lax.dot_general(weights, attended, NT, preferred_element_type=F32)
-
-        @pl.when(step == 2)
-        def _():
-            part[0] = quarters[2].astype(BF16)
-            far_up.start()
-            far_down.start()
-
-        @pl.when(step == 1)
-        def _():
-            part[1, high, :] = quarters[1, high, :].astype(BF16)
-            plain_up.start()
-
-        @pl.when(step == 3)
-        def _():
-            part[2, low, :] = quarters[3, low, :].astype(BF16)
-            plain_down.start()
+
+        @pl.loop(0, CHUNKS)
+        def _(c):
+            tokens = pl.ds(pl.multiple_of(c * HD, HD), HD)
+            attended = jnp.concatenate([attg[j, tokens, :] for j in range(4)], axis=1)
+            quarters[step, c] = lax.dot_general(weights, attended, NT, preferred_element_type=F32)
+
+            @pl.when(step == 2)
+            def _():
+                part[0, c] = quarters[2, c].astype(BF16)
+                far_up(c).start()
+                far_down(c).start()
+
+            @pl.when(step == 1)
+            def _():
+                part[1, c, high, :] = quarters[1, c, high, :].astype(BF16)
+                plain_up(c).start()
+
+            @pl.when(step == 3)
+            def _():
+                part[2, c, low, :] = quarters[3, c, low, :].astype(BF16)
+                plain_down(c).start()
 
         return code // 4
 
     lax.fori_loop(0, 4, quarter, other * rising + (1 - other) * falling)
 
-    far_up.wait_recv()
-    part[1, low, :] = (quarters[1, low, :] + far_in[0].astype(F32)).astype(BF16)
-    sum_up.start()
-    far_down.wait_recv()
-    part[2, high, :] = (quarters[3, high, :] + far_in[1].astype(F32)).astype(BF16)
-    sum_down.start()
-
-    def hand(k):
-        rows = pl.ds(k * HALF, HALF)
-        return pltpu.make_async_remote_copy(
-            res.at[rows], out_ref.at[rows], ss_h.at[k], rs_h.at[k],
+    @pl.loop(0, CHUNKS)
+    def _(c):
+        far_up(c).wait_recv()
+        part[1, c, low, :] = (quarters[1, c, low, :] + far_in[0, c].astype(F32)).astype(BF16)
+        sum_up(c).start()
+        far_down(c).wait_recv()
+        part[2, c, high, :] = (quarters[3, c, high, :] + far_in[1, c].astype(F32)).astype(BF16)
+        sum_down(c).start()
+
+    def hand(c):
+        tokens = pl.ds(pl.multiple_of(c * HD, HD), HD)
+        return pltpu.make_async_remote_copy(
+            res.at[c], out_ref.at[:, tokens], ss_h.at[c], rs_h.at[c],
             device_id=(lax.rem(section + 1, BLOCKS), t), device_id_type=MESH,
         )
 
-    for k, first, second in ((0, plain_down, sum_up), (1, plain_up, sum_down)):
-        first.wait_recv()
-        second.wait_recv()
-        rows = pl.ds(k * HALF, HALF)
-        mine_rows = pl.ds(pl.multiple_of(t * SHARE + k * HALF, HALF), HALF)
-        gate = columns[2, mine_rows, :]
-        for i in range(PATCH // HD):
-            tokens = pl.ds(i * HD, HD)
-            mixed = quarters[0, rows, tokens] + near_in[0, rows, tokens].astype(F32) + near_in[1, rows, tokens].astype(F32)
-            res[rows, tokens] = (xg[mine_rows, tokens].astype(F32) + gate * mixed).astype(BF16)
-        hand(k).start()
+    @pl.loop(0, CHUNKS)
+    def _(c):
+        for copy in (plain_up, plain_down, sum_up, sum_down):
+            copy(c).wait_recv()
+        tokens = pl.ds(pl.multiple_of(c * HD, HD), HD)
+        mixed = quarters[0, c] + near_in[0, c].astype(F32) + near_in[1, c].astype(F32)
+        gate = columns[2, my_features, :]
+        res[c] = (xg[my_features, tokens].astype(F32) + gate * mixed).astype(BF16)
+        hand(c).start()
 
     for p in range(4):
         view = wqkv.at[0, pl.ds(0, D - ROWS)]
@@ -372,10 +404,12 @@
         send_x(t, (section, t), ss_f.at[d]).wait_send()
     for d in range(3):
         send_a(x, d + 1, ss_a.at[d]).wait_send()
-    for copy in (far_up, far_down, plain_up, plain_down, sum_up, sum_down):
-        copy.wait_send()
-    for k in range(2):
-        hand(k).wait()
+
+    @pl.loop(0, CHUNKS)
+    def _(c):
+        for copy in (far_up, far_down, plain_up, plain_down, sum_up, sum_down):
+            copy(c).wait_send()
+        hand(c).wait()
 
 
 def local(block_weights, modulation, inflow, stale_cache, patch_index, assignment):
@@ -410,13 +444,13 @@
             pltpu.VMEM((4, PATCH, HD), BF16),
             pltpu.VMEM((N_TP, 2, PATCH), F32),
             pltpu.VMEM((8, PATCH), F32),
-            pltpu.VMEM((4, SHARE, PATCH), F32),
-            pltpu.VMEM((3, SHARE, PATCH), BF16),
-            pltpu.VMEM((2, HALF, PATCH), BF16),
-            pltpu.VMEM((2, SHARE, PATCH), BF16),
-            pltpu.VMEM((SHARE, PATCH), BF16),
+            pltpu.VMEM((4, CHUNKS, SHARE, HD), F32),
+            pltpu.VMEM((3, CHUNKS, SHARE, HD), BF16),
+            pltpu.VMEM((2, CHUNKS, HALF, HD), BF16),
+            pltpu.VMEM((2, CHUNKS, SHARE, HD), BF16),
+            pltpu.VMEM((CHUNKS, SHARE, HD), BF16),
             dma((4,)), dma((4,)), dma((3,)), dma((4,)), dma,
-            dma((6,)), dma((N_TP,)), dma((9,)), dma((3,)), dma((4,)), dma((6,)), dma((6,)), dma((2,)), dma((2,)),
+            dma((6,)), dma((N_TP,)), dma((9,)), dma((3,)), dma((4,)), dma((6, CHUNKS)), dma((6, CHUNKS)), dma((CHUNKS,)), dma((CHUNKS,)),
         ],
         compiler_params=pltpu.CompilerParams(
             collective_id=0, has_side_effects=True, vmem_limit_bytes=60 * 2**20

time: 116 us -> 113 us (0.974)
  Pallas kernels: 113 us -> 111 us
    pallas_call x1, Pallas kernels: 113 us -> 111 us  [local(): pl.pallas_call(kernel, out_shape=jax.ShapeDtypeStruct((SHARE, PATCH), BF1...]
where the time goes in v3:
time: 113 us
  Pallas kernels  111 us (98%)
  local copies, waits for them, and re-layouts  1.62 us (1%)
    pallas_call x1, Pallas kernels, local(): pl.pallas_call(kernel, out_shape=jax.ShapeDtypeStruct((SHARE, PATCH), BF1...  111 us

profile of v3, /device:TPU:1, one launch (start us, length us, event | category | flops | bytes accessed | tf_op | source)
XLA Modules:
  0.0 113.2 jit_solution(17836477124239582061)
XLA Ops:
  0.7 111.0 %shard_map.64 = bf16[192,512]{1,0:T(8,128)(2,1)} custom-call(s32[32]{0:T(128)} %assign_ref.1, s32[1]{0:T(128)S(6)} %copy.8.patch_ref, bf16[32,384,128]{2,1,0:T(8,128)(2,1)} %bitcast.9, f32[3,1,3072]{2,1,0:T(1,128)} %bitcast.13, bf16[192,512]{1,0:T(8,128)(2,1)} %bitcast.12, bf16[2,4,512,128]{3,2,1,0:T(8,128)(2,1)} %bitcast.10), custom_call_target="tpu_custom_call" | custom-call | tf_op jit(solution)/shard_map/pallas_call | solution.py:420
  111.6 1.6 %copy.9 = bf16[1,512,192]{1,2,0:T(8,128)(2,1)} copy(bf16[1,512,192]{1,2,0:T(8,128)(2,1)} %bitcast.11) | data formatting | bytes 393216

commit v4 on v3

--- a/solution.py
+++ b/solution.py
@@ -277,25 +277,23 @@
         o_stale[rows, :] = o_stale[rows, :] * (a_old * inverse)
         p_new[rows, :] = expo.astype(BF16)
 
+    def send_a(slot, c, e):
+        rows = pl.ds(pl.multiple_of(c * Q_STEP, Q_STEP), Q_STEP)
+        return pltpu.make_async_remote_copy(
+            attg.at[slot, rows], attg.at[slot, rows], ss_a.at[e - 1, c], rs_a.at[slot, c],
+            device_id=(section, lax.rem(x + e, 4) * 4 + zh), device_id_type=MESH,
+        )
+
     wait_weights(2)
     project(2, v_v)
 
-    @pl.loop(0, PATCH // Q_STEP)
-    def _(i):
-        rows = pl.ds(pl.multiple_of(i * Q_STEP, Q_STEP), Q_STEP)
+    @pl.loop(0, CHUNKS)
+    def _(c):
+        rows = pl.ds(pl.multiple_of(c * Q_STEP, Q_STEP), Q_STEP)
         fresh = jnp.dot(p_new[rows, :], v_v[...], preferred_element_type=F32)
         attg[x, rows, :] = (o_stale[rows, :] + fresh * m_new[rows, :]).astype(BF16)
-
-    def send_a(slot, e, sem):
-        return pltpu.make_async_remote_copy(
-            attg.at[slot], attg.at[slot], sem, rs_a.at[slot],
-            device_id=(section, lax.rem(x + e, 4) * 4 + zh), device_id_type=MESH,
-        )
-
-    for e in range(1, 4):
-        send_a(x, e, ss_a.at[e - 1]).start()
-    for e in range(1, 4):
-        send_a(lax.rem(x + e, 4), e, ss_a.at[e - 1]).wait_recv()
+        for e in range(1, 4):
+            send_a(x, c, e).start()
 
     def along(sign):
         return (section, x * 4 + lax.rem(zh + 4 + sign, 4))
@@ -325,14 +323,8 @@
     def sum_down(c):
         return remote(part.at[2, c, high], near_in.at[1, c, high], 5, c, -1)
 
-    at = lax.rem(y, 4)
-    rising = 228 - 3 * at - 84 * at * (at - 1) + 52 * at * (at - 1) * (at - 2)
-    falling = 27 + 48 * at + 33 * ((at * (at - 1)) // 2) - 7 * at * (at - 1) * (at - 2)
-    other = lax.rem(y // 4 + lax.rem(x, 2), 2)
-
-    def quarter(i, code):
-        group = lax.rem(code, 4)
-        step = lax.rem(group - zh + 4, 4)
+    for step in (2, 1, 3, 0):
+        group = lax.rem(zh + step, 4)
         features = pl.ds(pl.multiple_of(group * SHARE, SHARE), SHARE)
         view = wqkv.at[0, pl.ds(0, 8 * ROWS)]
         pltpu.make_async_copy(view, view, rs_o.at[group]).wait()
@@ -341,28 +333,25 @@
         @pl.loop(0, CHUNKS)
         def _(c):
             tokens = pl.ds(pl.multiple_of(c * HD, HD), HD)
+            if step == 2:
+                for e in range(1, 4):
+                    send_a(lax.rem(x + e, 4), c, e).wait_recv()
             attended = jnp.concatenate([attg[j, tokens, :] for j in range(4)], axis=1)
-            quarters[step, c] = lax.dot_general(weights, attended, NT, preferred_element_type=F32)
-
-            @pl.when(step == 2)
-            def _():
-                part[0, c] = quarters[2, c].astype(BF16)
+            value = lax.dot_general(weights, attended, NT, preferred_element_type=F32)
+            if step == 2:
+                part[0, c] = value.astype(BF16)
                 far_up(c).start()
                 far_down(c).start()
-
-            @pl.when(step == 1)
-            def _():
-                part[1, c, high, :] = quarters[1, c, high, :].astype(BF16)
+            elif step == 1:
+                quarters[1, c] = value
+                part[1, c, high, :] = value[HALF:].astype(BF16)
                 plain_up(c).start()
-
-            @pl.when(step == 3)
-            def _():
-                part[2, c, low, :] = quarters[3, c, low, :].astype(BF16)
+            elif step == 3:
+                quarters[2, c] = value
+                part[2, c, low, :] = value[:HALF].astype(BF16)
                 plain_down(c).start()
-
-        return code // 4
-
-    lax.fori_loop(0, 4, quarter, other * rising + (1 - other) * falling)
+            else:
+                quarters[0, c] = value
 
     @pl.loop(0, CHUNKS)
     def _(c):
@@ -370,7 +359,7 @@
         part[1, c, low, :] = (quarters[1, c, low, :] + far_in[0, c].astype(F32)).astype(BF16)
         sum_up(c).start()
         far_down(c).wait_recv()
-        part[2, c, high, :] = (quarters[3, c, high, :] + far_in[1, c].astype(F32)).astype(BF16)
+        part[2, c, high, :] = (quarters[2, c, high, :] + far_in[1, c].astype(F32)).astype(BF16)
         sum_down(c).start()
 
     def hand(c):
@@ -402,18 +391,17 @@
         send_x(t, (section, t), ss_x.at[d]).wait_send()
     for d in range(9):
         send_x(t, (section, t), ss_f.at[d]).wait_send()
-    for d in range(3):
-        send_a(x, d + 1, ss_a.at[d]).wait_send()
 
     @pl.loop(0, CHUNKS)
     def _(c):
         for copy in (far_up, far_down, plain_up, plain_down, sum_up, sum_down):
             copy(c).wait_send()
+        for e in range(1, 4):
+            send_a(x, c, e).wait_send()
         hand(c).wait()
 
 
 def local(block_weights, modulation, inflow, stale_cache, patch_index, assignment):
-    vmem = pl.BlockSpec(memory_space=pltpu.VMEM)
     smem = pl.BlockSpec(memory_space=pltpu.SMEM)
     hbm = pl.BlockSpec(memory_space=pltpu.HBM)
     dma = pltpu.SemaphoreType.DMA
@@ -421,7 +409,7 @@
         kernel,
         out_shape=jax.ShapeDtypeStruct((SHARE, PATCH), BF16),
         in_specs=[smem, smem, hbm, hbm, hbm, hbm],
-        out_specs=vmem,
+        out_specs=hbm,
         scratch_shapes=[
             pltpu.VMEM((BLOCKS, 4 * ROWS, HD), BF16),
             pltpu.VMEM((3, 1, D), F32),
@@ -444,13 +432,13 @@
             pltpu.VMEM((4, PATCH, HD), BF16),
             pltpu.VMEM((N_TP, 2, PATCH), F32),
             pltpu.VMEM((8, PATCH), F32),
-            pltpu.VMEM((4, CHUNKS, SHARE, HD), F32),
+            pltpu.VMEM((3, CHUNKS, SHARE, HD), F32),
             pltpu.VMEM((3, CHUNKS, SHARE, HD), BF16),
             pltpu.VMEM((2, CHUNKS, HALF, HD), BF16),
             pltpu.VMEM((2, CHUNKS, SHARE, HD), BF16),
             pltpu.VMEM((CHUNKS, SHARE, HD), BF16),
             dma((4,)), dma((4,)), dma((3,)), dma((4,)), dma,
-            dma((6,)), dma((N_TP,)), dma((9,)), dma((3,)), dma((4,)), dma((6, CHUNKS)), dma((6, CHUNKS)), dma((CHUNKS,)), dma((CHUNKS,)),
+            dma((6,)), dma((N_TP,)), dma((9,)), dma((3, CHUNKS)), dma((4, CHUNKS)), dma((6, CHUNKS)), dma((6, CHUNKS)), dma((CHUNKS,)), dma((CHUNKS,)),
         ],
         compiler_params=pltpu.CompilerParams(
             collective_id=0, has_side_effects=True, vmem_limit_bytes=60 * 2**20

time: 113 us -> 111 us (0.982)
  the two profiles are of different devices: /device:TPU:1 before, /device:TPU:24 now
where the time goes in v4:
time: 111 us
  Pallas kernels  109 us (98%)
  local copies, waits for them, and re-layouts  1.62 us (1%)
    pallas_call x1, Pallas kernels, local(): pl.pallas_call(kernel, out_shape=jax.ShapeDtypeStruct((SHARE, PATCH), BF1...  109 us

profile of v4, /device:TPU:24, one launch (start us, length us, event | category | flops | bytes accessed | tf_op | source)
XLA Modules:
  0.0 110.9 jit_solution(3553145522662497799)
XLA Ops:
  0.7 108.6 %shard_map.64 = bf16[192,512]{1,0:T(8,128)(2,1)} custom-call(s32[32]{0:T(128)} %assign_ref.1, s32[1]{0:T(128)S(6)} %copy.8.patch_ref, bf16[32,384,128]{2,1,0:T(8,128)(2,1)} %bitcast.9, f32[3,1,3072]{2,1,0:T(1,128)} %bitcast.13, bf16[192,512]{1,0:T(8,128)(2,1)} %bitcast.12, bf16[2,4,512,128]{3,2,1,0:T(8,128)(2,1)} %bitcast.10), custom_call_target="tpu_custom_call" | custom-call | tf_op jit(solution)/shard_map/pallas_call | solution.py:408
  109.2 1.6 %copy.9 = bf16[1,512,192]{1,2,0:T(8,128)(2,1)} copy(bf16[1,512,192]{1,2,0:T(8,128)(2,1)} %bitcast.11) | data formatting | bytes 393216

commit v5 on v4

--- a/solution.py
+++ b/solution.py
@@ -146,18 +146,18 @@
 
     for p in range(3):
         wqkv[p, my_rows, :] = send_w[BLOCKS - 1, pl.ds(p * ROWS, ROWS), :]
-    pass_on(1)
-    pass_on(3)
-
     @pl.loop(0, BLOCKS - 1)
     def _(k):
         send_part(k, 1).start()
 
-    pass_on(2)
+    pass_on(1)
+    pass_on(3)
 
     @pl.loop(0, BLOCKS - 1)
     def _(k):
         send_part(k, 2).start()
+
+    pass_on(2)
 
     @pl.loop(0, BLOCKS - 1)
     def _(k):

time: 111 us -> 110 us (level)
  the two profiles are of different devices: /device:TPU:24 before, /device:TPU:1 now
where the time goes in v5:
time: 110 us; the launch traced here: 108 us
  Pallas kernels  106 us (96%)
  local copies, waits for them, and re-layouts  1.62 us (1%)
    pallas_call x1, Pallas kernels, local(): pl.pallas_call(kernel, out_shape=jax.ShapeDtypeStruct((SHARE, PATCH), BF1...  106 us

profile of v5, /device:TPU:1, one launch (start us, length us, event | category | flops | bytes accessed | tf_op | source)
XLA Modules:
  0.0 108.2 jit_solution(17513415617548569900)
XLA Ops:
  0.7 105.9 %shard_map.64 = bf16[192,512]{1,0:T(8,128)(2,1)} custom-call(s32[32]{0:T(128)} %assign_ref.1, s32[1]{0:T(128)S(6)} %copy.8.patch_ref, bf16[32,384,128]{2,1,0:T(8,128)(2,1)} %bitcast.9, f32[3,1,3072]{2,1,0:T(1,128)} %bitcast.13, bf16[192,512]{1,0:T(8,128)(2,1)} %bitcast.12, bf16[2,4,512,128]{3,2,1,0:T(8,128)(2,1)} %bitcast.10), custom_call_target="tpu_custom_call" | custom-call | tf_op jit(solution)/shard_map/pallas_call | solution.py:408
  106.6 1.6 %copy.9 = bf16[1,512,192]{1,2,0:T(8,128)(2,1)} copy(bf16[1,512,192]{1,2,0:T(8,128)(2,1)} %bitcast.11) | data formatting | bytes 393216

commit v6 on v5

--- a/solution.py
+++ b/solution.py
@@ -285,13 +285,13 @@
         )
 
     wait_weights(2)
-    project(2, v_v)
+    v_v[...] = jnp.dot(normed[...], wqkv[2], preferred_element_type=F32).astype(BF16)
+
+    fresh = jnp.dot(p_new[...], v_v[...], preferred_element_type=F32)
+    attg[x] = (o_stale[...] + fresh * m_new[...]).astype(BF16)
 
     @pl.loop(0, CHUNKS)
     def _(c):
-        rows = pl.ds(pl.multiple_of(c * Q_STEP, Q_STEP), Q_STEP)
-        fresh = jnp.dot(p_new[rows, :], v_v[...], preferred_element_type=F32)
-        attg[x, rows, :] = (o_stale[rows, :] + fresh * m_new[rows, :]).astype(BF16)
         for e in range(1, 4):
             send_a(x, c, e).start()
 

time: 110 us -> 109 us (level)
  no operation moved by 1% of the time
where the time goes in v6:
time: 109 us; the launch traced here: 108 us
  Pallas kernels  105 us (96%)
  local copies, waits for them, and re-layouts  1.62 us (1%)
    pallas_call x1, Pallas kernels, local(): pl.pallas_call(kernel, out_shape=jax.ShapeDtypeStruct((SHARE, PATCH), BF1...  105 us

profile of v6, /device:TPU:1, one launch (start us, length us, event | category | flops | bytes accessed | tf_op | source)
XLA Modules:
  0.0 107.6 jit_solution(6341012750428285701)
XLA Ops:
  0.7 105.3 %shard_map.64 = bf16[192,512]{1,0:T(8,128)(2,1)} custom-call(s32[32]{0:T(128)} %assign_ref.1, s32[1]{0:T(128)S(6)} %copy.8.patch_ref, bf16[32,384,128]{2,1,0:T(8,128)(2,1)} %bitcast.9, f32[3,1,3072]{2,1,0:T(1,128)} %bitcast.13, bf16[192,512]{1,0:T(8,128)(2,1)} %bitcast.12, bf16[2,4,512,128]{3,2,1,0:T(8,128)(2,1)} %bitcast.10), custom_call_target="tpu_custom_call" | custom-call | tf_op jit(solution)/shard_map/pallas_call | solution.py:408
  106.0 1.6 %copy.9 = bf16[1,512,192]{1,2,0:T(8,128)(2,1)} copy(bf16[1,512,192]{1,2,0:T(8,128)(2,1)} %bitcast.11) | data formatting | bytes 393216
